TPU v7x, 512 devices: a whole 4x4x16 slice. The times are simulated.
512 devices in a mesh: view: 32 (over z, x_lo), slab: 16 (over x_hi, y, core).
Axes of the slice: x: 4 (x_hi: 2, x_lo: 2; x = x_hi * 2 + x_lo), y: 4, z: 16, core: 2. Of those that a mesh axis runs over, the one named last changes fastest.
Arguments:
- projections: bfloat16 [256, 64, 736], P('view', 'slab'), may hold values from -24 to 24
- conj_index: int32 [256], P('view'), may hold values from 0 to 7
- conj_weight: float32 [256, 736], P('view'), may hold values from 0.1 to 0.9
- row_index: int32 [256, 16, 256], P('view', None, 'slab'), may hold values from 0 to 7
- col_index: int32 [256, 16384], P('view'), may hold values from 0 to 734
- col_frac: int32 [256, 16384], P('view'), may hold values from 0 to 255
Outputs:
- image: float32 [256, 16384], P('slab', 'view')
All inputs are finite; a program needn't handle non-finite values.
Results may differ from a plain program's by a relative error of at most 0.0051.
Values may be sent and summed in bfloat16 or wider, within the bound.
A program may use at most 64 MiB of HBM per device.

v0:
```python
import math

import jax
import jax.numpy as jnp
from jax import lax
from jax.sharding import PartitionSpec as P

RIM = 2


def passed_along(block, axis, distance):
    devices = range(lax.axis_size(axis))
    route = [((i - distance) % len(devices), i) for i in devices]
    return lax.ppermute(block, axis, route)


def with_halo(block, sides, width):
    for axis, dim in sides:
        count = lax.axis_size(axis)
        forward = [(i, i + 1) for i in range(count - 1)]
        backward = [(target, source) for source, target in forward]
        low = lax.ppermute(
            lax.slice_in_dim(block, block.shape[dim] - width, None, axis=dim), axis, forward
        )
        high = lax.ppermute(lax.slice_in_dim(block, 0, width, axis=dim), axis, backward)
        block = jnp.concatenate([low, block, high], axis=dim)
    return block


def ramp_matrix(width):
    place = jnp.arange(width, dtype=jnp.int32)
    offset = place[None, :] - place[:, None]
    square = (offset * offset).astype(jnp.float32)
    odd_term = -1.0 / (math.pi * math.pi * jnp.maximum(square, 1.0))
    values = jnp.where(offset == 0, 0.25, jnp.where(offset % 2 != 0, odd_term, 0.0))
    return values.astype(jnp.bfloat16)


def apply_ramp(rows_in, ramp):
    lead, count, width = rows_in.shape
    flat = rows_in.reshape(lead * count, width)
    return (
        jnp.dot(flat, ramp, preferred_element_type=jnp.float32)
        .astype(jnp.bfloat16)
        .reshape(lead, count, width)
    )


def on_device(projections, conj_index, conj_weight, row_index, col_index, col_frac):
    n_view = lax.axis_size("view")
    v_dev, r_dev, width = projections.shape
    partner = passed_along(projections, "view", n_view // 2)
    mirror = jnp.take(partner, conj_index, axis=0)[:, :, ::-1].astype(jnp.float32)
    weight = conj_weight[:, None, :]
    blended = ((1.0 - weight) * projections.astype(jnp.float32) + weight * mirror).astype(
        jnp.bfloat16
    )
    ramp = ramp_matrix(width)
    band = with_halo(apply_ramp(blended, ramp), (("slab", 1),), RIM)
    img_rows = row_index.shape[1]
    z_dev = row_index.shape[2]
    pix = col_index.shape[1]
    img_cols = pix // img_rows
    columns = col_index.reshape(v_dev, img_rows, img_cols)
    fraction = (col_frac.astype(jnp.float32) / 256.0).reshape(v_dev, img_rows, img_cols)
    detector = jnp.arange(width, dtype=jnp.int32)[:, None]

    def tile_step(tile, total):
        part = jnp.zeros((z_dev, img_cols), jnp.float32)
        for view_no in range(v_dev):
            rows_now = lax.dynamic_index_in_dim(row_index[view_no], tile, 0, keepdims=False)
            picked = jnp.take(band[view_no], rows_now, axis=0)
            left = lax.dynamic_index_in_dim(columns[view_no], tile, 0, keepdims=False)[None, :]
            share = lax.dynamic_index_in_dim(fraction[view_no], tile, 0, keepdims=False)[None, :]
            onehot = jnp.where(detector == left, 1.0 - share, 0.0) + jnp.where(
                detector == left + 1, share, 0.0
            )
            part = part + jnp.dot(
                picked, onehot.astype(jnp.bfloat16), preferred_element_type=jnp.float32
            )
        return lax.dynamic_update_slice_in_dim(total, part, tile * img_cols, 1)

    partial_image = lax.fori_loop(0, img_rows, tile_step, jnp.zeros((z_dev, pix), jnp.float32))
    factor = 1.0 / math.sqrt(v_dev * n_view)
    whole = lax.psum(partial_image, "view")
    width_share = pix // n_view
    summed = lax.dynamic_slice_in_dim(whole, lax.axis_index("view") * width_share, width_share, 1)
    return summed * factor


def solution(mesh):
    return jax.shard_map(
        on_device,
        mesh=mesh,
        in_specs=(
            P("view", "slab", None),
            P("view"),
            P("view", None),
            P("view", None, "slab"),
            P("view", None),
            P("view", None),
        ),
        out_specs=P("slab", "view"),
        check_vma=False,
    )
```

profile of v0, /device:TPU:6, one launch (start us, length us, event | category | flops | bytes accessed | tf_op | source)
XLA Modules:
  0.0 494.6 jit_solution(7701755911453112406)
XLA Ops:
  6.5 15.7 %collective-permute-start = (bf16[8,4,736]{2,1,0:T(4,128)(2,1)}, bf16[8,4,736]{2,1,0:T(4,128)(2,1)S(1)}, u32[]{:S(2)}, u32[]{:S(2)}) collective-permute-start(bf16[8,4,736]{2,1,0:T(4,128)(2,1)} %param.10), channel_id=1, source_target_pairs={{256,0},{272,16},{288,32},{304,48},{320,64},{336,80},{352,96},{368... | collective-permute-start | bytes 141320 | tf_op jit(solution)/shard_map/ppermute | solution.py:14
  23.6 0.7 broadcast_subtract_fusion.8
  24.3 1.2 collective-permute-done
  26.9 0.9 add_convert_fusion.32
  27.8 1.2 fusion.73
  29.1 3.9 collective-permute-start.2
  33.0 1.9 collective-permute-start.1
  35.6 6.1 %collective-permute-done.1 = bf16[8,2,736]{2,1,0:T(2,128)(2,1)S(1)} collective-permute-done((bf16[8,2,736]{2,1,0:T(2,128)(2,1)S(1)}, bf16[8,2,736]{2,1,0:T(2,128)(2,1)S(1)}, u32[]{:S(2)}, u32[]{:S(2)}) %collective-permute-start.1) | collective-permute-done | bytes 23584 | tf_op jit(solution)/shard_map/ppermute | solution.py:22
  41.9 180.3 %while.15 = (s32[]{:T(128)}, f32[16,16384]{1,0:T(8,128)S(1)}, bf16[8,8,736]{2,1,0:T(8,128)(2,1)S(1)}, s32[8,16,16]{2,1,0:T(8,128)S(1)}, s32[8,16,1024]{2,1,0:T(8...) while((s32[]{:T(128)}, f32[16,16384]{1,0:T(8,128)S(1)}, ...), condition=%wide.region_1.3_spmd.clone.clone, body=%wide.region_0.0_spmd.clone.clone.sunk | while | flops 229348096 | bytes 4280255 | solution.py:83
  45.6 0.7 fusion.119
  52.5 0.7 fusion.124
  63.8 0.7 fusion.124
  72.2 0.7 fusion.122
  75.0 0.7 fusion.124
  84.9 0.7 fusion.123
  86.3 0.7 fusion.124
  93.4 0.7 fusion.121
  97.6 0.7 fusion.124
  108.8 0.7 fusion.124
  120.1 0.7 fusion.124
  131.4 0.7 fusion.124
  142.6 0.7 fusion.124
  153.9 0.7 fusion.124
  165.2 0.7 fusion.124
  176.4 0.7 fusion.124
  187.7 0.7 fusion.124
  199.0 0.7 fusion.124
  210.2 0.7 fusion.124
  221.5 0.7 fusion.124
  222.2 1.0 copy-done
  223.2 263.2 %all-reduce.2.cloned.1.call-done = f32[16,16384]{1,0:T(8,128)} async-done(((f32[16,16384]{1,0:T(8,128)}), f32[16,16384]{1,0:T(8,128)}) %all-reduce.2.cloned.1.call-update) | async-done | bytes 1048592 | tf_op jit(solution)/shard_map/psum | solution.py:85
  486.4 1.4 dynamic-slice_multiply_fusion
  (900 shorter events, 164.8 us)
Async XLA Ops:
  6.5 479.8 %all-reduce.2.cloned.1.call-start = ((), (), s32[]{:S(2)}) async-start(), calls=%async_computation | async-start | bytes 2097152 | tf_op jit(solution)/shard_map/psum | solution.py:85
  6.5 19.0 %collective-permute-start = (bf16[8,4,736]{2,1,0:T(4,128)(2,1)}, bf16[8,4,736]{2,1,0:T(4,128)(2,1)S(1)}, u32[]{:S(2)}, u32[]{:S(2)}) collective-permute-start(bf16[8,4,736]{2,1,0:T(4,128)(2,1)} %param.10), channel_id=1, source_target_pairs={{256,0},{272,16},{288,32},{304,48},{320,64},{336,80},{352,96},{368... | collective-permute-start | bytes 141320 | tf_op jit(solution)/shard_map/ppermute | solution.py:14
  27.8 7.1 %copy-start.2 = (s32[8,16384]{1,0:T(8,128)S(1)}, s32[8,16384]{1,0:T(8,128)}, u32[]{:S(2)}) copy-start(s32[8,16384]{1,0:T(8,128)} %param.15) | copy-start | bytes 1572868
  29.0 6.0 %copy-start.3 = (s32[8,16384]{1,0:T(8,128)S(1)}, s32[8,16384]{1,0:T(8,128)}, u32[]{:S(2)}) copy-start(s32[8,16384]{1,0:T(8,128)} %param.14) | copy-start | bytes 1572868
  29.1 6.5 %collective-permute-start.2 = (bf16[8,2,736]{2,1,0:T(2,128)(2,1)S(1)}, bf16[8,2,736]{2,1,0:T(2,128)(2,1)S(1)}, u32[]{:S(2)}, u32[]{:S(2)}) collective-permute-start(bf16[8,2,736]{2,1,0:T(2,128)(2,1)S(1)} %get-tuple-element.307), channel_id=1, source_target_pairs={{1,0},{2,1},{3,2},{4,3},{5,4},{6,5},{7,6},{8,7},{9,8},{10,9},{11,1... | collective-permute-start | bytes 70664 | tf_op jit(solution)/shard_map/ppermute | solution.py:25
  33.0 8.8 %collective-permute-start.1 = (bf16[8,2,736]{2,1,0:T(2,128)(2,1)S(1)}, bf16[8,2,736]{2,1,0:T(2,128)(2,1)S(1)}, u32[]{:S(2)}, u32[]{:S(2)}) collective-permute-start(bf16[8,2,736]{2,1,0:T(2,128)(2,1)S(1)} %get-tuple-element.306), channel_id=1, source_target_pairs={{0,1},{1,2},{2,3},{3,4},{4,5},{5,6},{6,7},{7,8},{8,9},{9,10},{10,1... | collective-permute-start | bytes 70664 | tf_op jit(solution)/shard_map/ppermute | solution.py:22
  35.3 6.6 %copy-start.1 = (s32[8,16,16]{2,1,0:T(8,128)S(1)}, s32[8,16,16]{2,1,0:T(8,128)}, u32[]{:S(2)}) copy-start(s32[8,16,16]{2,1,0:T(8,128)} %param.13) | copy-start | bytes 24580
  222.2 1.0 copy-start
Sparse Core Ops, SparseCore 0:
  223.3 262.9 all-reduce.1
where the time goes:
time: 496 us; the launch traced here: 495 us
  waiting for transfers between devices  270 us (54%)
  matrix products  95.6 us (19%)
  local copies, waits for them, and re-layouts  81.9 us (17%)
  starting transfers between devices  21.5 us (4%)
  between operations  13.5 us (3%)
  other arithmetic  7.32 us (1%)
    psum x1, waiting for transfers between devices, on_device(): whole = lax.psum(partial_image, 'view')  263 us
    dot_general x128, matrix products, tile_step(): jnp.dot(picked, onehot.astype(jnp.bfloat16), preferred_element_type=jnp.f...  94.4 us
    gather x128, local copies, waits for them, and re-layouts, tile_step(): picked = jnp.take(band[view_no], rows_now, axis=0)  75.6 us
    ppermute x1, starting transfers between devices, passed_along(): return lax.ppermute(block, axis, route)  15.7 us
  transfers between devices with their start and end apart: 4, of which 3 were waited for; matrix products, arithmetic and copies ran while one was open for 1% of the time, Pallas kernels for 0%

commit v1 on v0

v1 whole, which is shorter than its diff:
```python
import math

import jax
import jax.numpy as jnp
from jax import lax
from jax.experimental import pallas as pl
from jax.experimental.pallas import tpu as pltpu
from jax.sharding import PartitionSpec as P

MESH = pl.DeviceIdType.MESH
BF16 = jnp.bfloat16
F32 = jnp.float32

V = 8
R = 4
W = 736
NZ = 16
TILE = 1024
HALF = TILE // 2
STEP = 6
PARTS = STEP + 1
LANES = 128
LAG = 4


def iota(shape, dim):
    return lax.broadcasted_iota(jnp.int32, shape, dim)


def hat(distance):
    return jnp.maximum(1.0 - jnp.abs(distance), 0.0)


def kernel(
    conj_ref,
    proj_hbm,
    weight_hbm,
    rows_hbm,
    col_hbm,
    frac_hbm,
    out_ref,
    proj,
    weight,
    rowidx,
    col,
    frac,
    stage,
    mine,
    theirs,
    mirrored,
    mirror_weight,
    ramp,
    band,
    lhs,
    coarse,
    fine,
    pick,
    planes,
    part,
    own,
    x_out,
    x_in,
    z_out,
    z_in,
    load_sem,
    pair_sem,
    halo_send,
    halo_recv,
    x_send,
    x_recv,
    z_send,
    z_recv,
):
    view, slab = lax.axis_index("view"), lax.axis_index("slab")
    z, x_lo = view // 2, lax.rem(view, 2)
    last = lax.axis_size("slab") - 1

    def at(zz, xx):
        return (zz * 2 + xx, slab)

    def z_peer(distance):
        return lax.rem(z + distance, NZ)

    loads = [
        pltpu.make_async_copy(src, dst, load_sem.at[i])
        for i, (src, dst) in enumerate(
            ((proj_hbm, proj), (weight_hbm, weight), (rows_hbm, rowidx), (col_hbm, col), (frac_hbm, frac))
        )
    ]
    for load in loads:
        load.start()

    barrier = pltpu.get_barrier_semaphore()

    def greet(d, carry):
        pl.semaphore_signal(barrier, inc=1, device_id=at(z_peer(d), x_lo), device_id_type=MESH)
        return carry

    lax.fori_loop(1, NZ, greet, 0)
    pl.semaphore_signal(barrier, inc=1, device_id=at(z, 1 - x_lo), device_id_type=MESH)

    @pl.when(slab > 0)
    def _():
        pl.semaphore_signal(barrier, inc=1, device_id=(view, slab - 1), device_id_type=MESH)

    @pl.when(slab < last)
    def _():
        pl.semaphore_signal(barrier, inc=1, device_id=(view, slab + 1), device_id_type=MESH)

    loads[0].wait()
    for v in range(V):
        rows = proj[v].astype(F32)
        for r in range(R):
            stage[r * V + v : r * V + v + 1, :] = rows[r : r + 1]
    mine[...] = stage[...].astype(BF16)

    loads[3].wait()
    loads[4].wait()

    def prepare(tile, carry):
        off = pl.multiple_of(tile * TILE, TILE)
        k = col[:, pl.ds(off, TILE)].astype(F32)
        a = jnp.floor((k + 0.5) * (1.0 / STEP))
        place = k - a * STEP + frac[:, pl.ds(off, TILE)].astype(F32) * (1.0 / 256.0)
        for b in range(PARTS):
            fine[b, :, pl.ds(off, TILE)] = hat(place - b)
        lanes = iota((LANES, TILE), 0).astype(F32).astype(BF16)
        for v in range(V):
            coarse[v, :, pl.ds(off, TILE)] = hat(lanes - a[v : v + 1, :].astype(BF16)).astype(BF16)
        return carry

    lax.fori_loop(0, NZ // 2, prepare, 0)

    pl.semaphore_wait(
        barrier, NZ + (slab > 0).astype(jnp.int32) + (slab < last).astype(jnp.int32)
    )
    pair = pltpu.make_async_remote_copy(
        src_ref=mine,
        dst_ref=theirs,
        send_sem=pair_sem.at[0],
        recv_sem=pair_sem.at[1],
        device_id=at(z_peer(NZ // 2), x_lo),
        device_id_type=MESH,
    )
    pair.start()

    lax.fori_loop(NZ // 2, NZ, prepare, 0)

    for b in range(PARTS):
        column = STEP * iota((W, LANES), 1) + b
        offset = column + iota((W, LANES), 0) - (W - 1)
        square = (offset * offset).astype(F32)
        odd = -1.0 / (math.pi * math.pi * jnp.maximum(square, 1.0))
        value = jnp.where(offset == 0, 0.25, jnp.where((offset & 1) == 1, odd, 0.0))
        ramp[:, b * LANES : (b + 1) * LANES] = jnp.where(column < W, value, 0.0).astype(BF16)

    flip = jnp.where(iota((W, W), 0) + iota((W, W), 1) == W - 1, 1.0, 0.0).astype(BF16)
    mirrored[...] = jnp.dot(mine[...], flip, preferred_element_type=F32)
    loads[1].wait()
    whole = weight[...]
    high = whole.astype(BF16).astype(F32)
    middle = (whole - high).astype(BF16).astype(F32)
    low = (whole - high - middle).astype(BF16).astype(F32)
    split = jnp.concatenate([high, middle, low], axis=0).astype(BF16)
    flipped = jnp.dot(split, flip, preferred_element_type=F32)
    mirror_weight[...] = flipped[0:V] + flipped[V : 2 * V] + flipped[2 * V : 3 * V]

    loads[2].wait()
    for t in range(NZ):
        blocks = []
        for v in range(V):
            wanted = jnp.broadcast_to(rowidx[v, t : t + 1, :], (2 * R, NZ))
            blocks.append(jnp.where(wanted == iota((2 * R, NZ), 0), 1.0, 0.0))
        pick[t] = jnp.concatenate(blocks, axis=0).T.astype(BF16)

    row, other = iota((V * R, V * R), 0), iota((V * R, V * R), 1)
    conj = jnp.zeros((V * R, V * R), jnp.int32)
    for v in range(V):
        conj = jnp.where((row & (V - 1)) == v, conj_ref[v], conj)
    same_row = (row >> 3) == (other >> 3)
    select = jnp.where(jnp.logical_and(same_row, (other & (V - 1)) == conj), 1.0, 0.0).astype(BF16)
    share = jnp.concatenate([mirror_weight[...]] * R, axis=0)
    kept = (1.0 - share) * mirrored[...]
    pair.wait_recv()
    chosen = jnp.dot(select, theirs[...], preferred_element_type=F32)
    blended = (kept + share * chosen).astype(BF16)
    band[2 * V : (2 + R) * V, :] = jnp.dot(blended, ramp[...], preferred_element_type=F32).astype(BF16)

    halo = 2 * V
    down = pltpu.make_async_remote_copy(
        src_ref=band.at[pl.ds(halo, halo)],
        dst_ref=band.at[pl.ds(halo + R * V, halo)],
        send_sem=halo_send.at[0],
        recv_sem=halo_recv.at[0],
        device_id=(view, jnp.maximum(slab - 1, 0)),
        device_id_type=MESH,
    )
    up = pltpu.make_async_remote_copy(
        src_ref=band.at[pl.ds(2 * halo, halo)],
        dst_ref=band.at[pl.ds(0, halo)],
        send_sem=halo_send.at[1],
        recv_sem=halo_recv.at[1],
        device_id=(view, jnp.minimum(slab + 1, last)),
        device_id_type=MESH,
    )

    @pl.when(slab > 0)
    def _():
        down.start()

    @pl.when(slab < last)
    def _():
        up.start()

    @pl.when(slab == 0)
    def _():
        band[0:halo, :] = jnp.zeros((halo, PARTS * LANES), BF16)

    @pl.when(slab == last)
    def _():
        band[halo + R * V :, :] = jnp.zeros((halo, PARTS * LANES), BF16)

    @pl.when(slab < last)
    def _():
        down.wait_recv()

    @pl.when(slab > 0)
    def _():
        up.wait_recv()

    count = 2 * R * V
    to, source = iota((count, count), 0), iota((count, count), 1)
    order = jnp.where(source == (to & 7) * V + (to >> 3), 1.0, 0.0).astype(BF16)
    by_view = jnp.dot(order, band[...], preferred_element_type=F32)
    for v in range(V):
        lhs[v] = jnp.concatenate(
            [by_view[v * 2 * R : (v + 1) * 2 * R, b * LANES : (b + 1) * LANES] for b in range(PARTS)],
            axis=0,
        ).astype(BF16)

    def tile_of(n):
        return lax.rem(z + NZ // 2 + (1 - 2 * lax.rem(n, 2)) * ((n + 1) // 2), NZ)

    def x_copy(tile):
        return pltpu.make_async_remote_copy(
            src_ref=x_out.at[tile],
            dst_ref=x_in.at[tile],
            send_sem=x_send.at[tile],
            recv_sem=x_recv.at[tile],
            device_id=at(z, 1 - x_lo),
            device_id_type=MESH,
        )

    def z_copy(tile, slot):
        return pltpu.make_async_remote_copy(
            src_ref=z_out.at[tile],
            dst_ref=z_in.at[slot],
            send_sem=z_send.at[tile],
            recv_sem=z_recv.at[slot],
            device_id=at(tile, x_lo),
            device_id_type=MESH,
        )

    def compute(n):
        tile = tile_of(n)
        off = pl.multiple_of(tile * TILE, TILE)
        for v in range(V):
            columns = jnp.dot(lhs[v], coarse[v, :, pl.ds(off, TILE)], preferred_element_type=F32)
            total = None
            for b in range(PARTS):
                weights = jnp.broadcast_to(fine[b, v : v + 1, pl.ds(off, TILE)], (2 * R, TILE))
                term = columns[b * 2 * R : (b + 1) * 2 * R] * weights
                total = term if total is None else total + term
            planes[v * 2 * R : (v + 1) * 2 * R, :] = total
        part[...] = jnp.dot(pick[tile], planes[...].astype(BF16), preferred_element_type=F32)
        theirs_at = pl.multiple_of((1 - x_lo) * HALF, HALF)
        x_out[tile] = part[:, pl.ds(theirs_at, HALF)].astype(BF16)
        x_copy(tile).start()
        own[tile] = part[:, pl.ds(pl.multiple_of(x_lo * HALF, HALF), HALF)]

    def pass_on(n):
        tile = tile_of(n)
        x_copy(tile).wait_recv()
        z_out[tile] = (own[tile] + x_in[tile].astype(F32)).astype(BF16)
        z_copy(tile, z).start()

    def first(n, carry):
        compute(n)
        return carry

    def middle_steps(n, carry):
        compute(n)
        pass_on(n - LAG)
        return carry

    def tail(n, carry):
        pass_on(n)
        return carry

    lax.fori_loop(0, LAG, first, 0)
    lax.fori_loop(LAG, NZ, middle_steps, 0)
    lax.fori_loop(NZ - LAG, NZ - 1, tail, 0)
    x_copy(z).wait_recv()
    part[:, 0:HALF] = own[z] + x_in[z].astype(F32)

    def gather(d, carry):
        peer = z_peer(d)
        z_copy(peer, peer).wait_recv()
        part[:, 0:HALF] += z_in[peer].astype(F32)
        return carry

    lax.fori_loop(1, NZ, gather, 0)
    out_ref[...] = part[:, 0:HALF] * (1.0 / math.sqrt(V * lax.axis_size("view")))

    pair.wait_send()

    @pl.when(slab > 0)
    def _():
        down.wait_send()

    @pl.when(slab < last)
    def _():
        up.wait_send()

    def sent(d, carry):
        peer = z_peer(d)
        x_copy(peer).wait_send()
        z_copy(peer, z).wait_send()
        return carry

    lax.fori_loop(1, NZ, sent, 0)
    x_copy(z).wait_send()


def on_device(projections, conj_index, conj_weight, row_index, col_index, col_frac):
    pix = NZ * TILE
    anywhere = pl.BlockSpec(memory_space=pl.ANY)
    dma = pltpu.SemaphoreType.DMA
    return pl.pallas_call(
        kernel,
        out_shape=jax.ShapeDtypeStruct((NZ, HALF), F32),
        in_specs=[pl.BlockSpec(memory_space=pltpu.SMEM)] + [anywhere] * 5,
        out_specs=pl.BlockSpec(memory_space=pltpu.VMEM),
        scratch_shapes=[
            pltpu.VMEM((V, R, W), BF16),
            pltpu.VMEM((V, W), F32),
            pltpu.VMEM((V, NZ, NZ), jnp.int32),
            pltpu.VMEM((V, pix), jnp.int32),
            pltpu.VMEM((V, pix), jnp.int32),
            pltpu.VMEM((V * R, W), F32),
            pltpu.VMEM((V * R, W), BF16),
            pltpu.VMEM((V * R, W), BF16),
            pltpu.VMEM((V * R, W), F32),
            pltpu.VMEM((V, W), F32),
            pltpu.VMEM((W, PARTS * LANES), BF16),
            pltpu.VMEM((2 * R * V, PARTS * LANES), BF16),
            pltpu.VMEM((V, PARTS * 2 * R, LANES), BF16),
            pltpu.VMEM((V, LANES, pix), BF16),
            pltpu.VMEM((PARTS, V, pix), F32),
            pltpu.VMEM((NZ, NZ, 2 * R * V), BF16),
            pltpu.VMEM((2 * R * V, TILE), F32),
            pltpu.VMEM((NZ, TILE), F32),
            pltpu.VMEM((NZ, NZ, HALF), F32),
            pltpu.VMEM((NZ, NZ, HALF), BF16),
            pltpu.VMEM((NZ, NZ, HALF), BF16),
            pltpu.VMEM((NZ, NZ, HALF), BF16),
            pltpu.VMEM((NZ, NZ, HALF), BF16),
            dma((5,)),
            dma((2,)),
            dma((2,)),
            dma((2,)),
            dma((NZ,)),
            dma((NZ,)),
            dma((NZ,)),
            dma((NZ,)),
        ],
        compiler_params=pltpu.CompilerParams(
            collective_id=0, has_side_effects=True, vmem_limit_bytes=56 * 2**20
        ),
        name="backproject",
    )(conj_index, projections, conj_weight, row_index, col_index, col_frac)


def solution(mesh):
    return jax.shard_map(
        on_device,
        mesh=mesh,
        in_specs=(
            P("view", "slab", None),
            P("view"),
            P("view", None),
            P("view", None, "slab"),
            P("view", None),
            P("view", None),
        ),
        out_specs=P("slab", "view"),
        check_vma=False,
    )
```

time: 496 us -> 48.2 us (0.10)
  the two profiles are of different devices: /device:TPU:6 before, /device:TPU:5 now
where the time goes in v1:
time: 48.2 us; the launch traced here: 48 us
  Pallas kernels  46.6 us (97%)
  local copies, waits for them, and re-layouts  1.38 us (3%)
    pallas_call x1, Pallas kernels, on_device(): pl.pallas_call(kernel, out_shape=jax.ShapeDtypeStruct((NZ, HALF), F32), i...  46.6 us
    unnamed x1, local copies, waits for them, and re-layouts  1.38 us

profile of v1, /device:TPU:5, one launch (start us, length us, event | category | flops | bytes accessed | tf_op | source)
XLA Modules:
  0.0 48.0 jit_solution(6350468536982492215)
XLA Ops:
  0.0 46.6 %backproject.1 = f32[16,512]{1,0:T(8,128)} custom-call(s32[8]{0:T(128)} %conj_ref.1, bf16[8,4,736]{2,1,0:T(4,128)(2,1)} %proj_hbm.1, f32[8,736]{1,0:T(8,128)} %weight_hbm.1, s32[8,16,16]{2,1,0:T(8,128)} %rows_hbm.1, s32[8,16384]{1,0:T(8,128)} %col_hbm.1, s32[8,16384]{1,0:T(8,128)} %frac_hbm.1), custom_call_target="tpu_custom_call" | custom-call | tf_op jit(solution)/shard_map/backproject/pallas_call | solution.py:339
  46.6 1.4 %copy.8 = f32[16,512]{1,0:T(8,128)} copy(f32[16,512]{1,0:T(8,128)} %backproject.1) | data formatting | bytes 65536

commit v2 on v1

v2 whole, which is shorter than its diff:
```python
import math

import jax
import jax.numpy as jnp
from jax import lax
from jax.experimental import pallas as pl
from jax.experimental.pallas import tpu as pltpu
from jax.sharding import PartitionSpec as P

MESH = pl.DeviceIdType.MESH
BF16 = jnp.bfloat16
F32 = jnp.float32

V = 8
R = 4
W = 736
NZ = 16
TILE = 1024
HALF = TILE // 2
STEP = 6
PARTS = STEP + 1
LANES = 128
REACH = 4
FAR = NZ // 2 - 1


def iota(shape, dim):
    return lax.broadcasted_iota(jnp.int32, shape, dim)


def hat(distance):
    return jnp.maximum(1.0 - jnp.abs(distance), 0.0)


def kernel(
    conj_hbm,
    proj_hbm,
    weight_hbm,
    rows_hbm,
    col_hbm,
    frac_hbm,
    out_ref,
    conj_ref,
    proj,
    weight,
    rowidx,
    col,
    frac,
    stage,
    mine,
    theirs,
    kept,
    mirror_weight,
    ramp,
    edge,
    edge_in,
    band,
    lhs,
    coarse,
    fine,
    pick,
    planes,
    part,
    own,
    block,
    x_in,
    relay_in,
    z_in,
    load_sem,
    pair_sem,
    halo_send,
    halo_recv,
    block_send,
    x_recv,
    relay_recv,
    z_recv,
):
    view, slab = lax.axis_index("view"), lax.axis_index("slab")
    z, x_lo = view // 2, lax.rem(view, 2)
    last = lax.axis_size("slab") - 1

    def at(zz, xx):
        return (zz * 2 + xx, slab)

    def z_peer(distance):
        return lax.rem(z + distance, NZ)

    barrier = pltpu.get_barrier_semaphore()

    def greet(*device):
        pl.semaphore_signal(barrier, inc=1, device_id=device, device_id_type=MESH)

    def greet_z(d, carry):
        for x in range(2):
            greet(*at(z_peer(d), x))
            greet(*at(z_peer(NZ - d), x))
        return carry

    partner = at(z_peer(NZ // 2), x_lo)
    greet(*partner)
    lax.fori_loop(1, REACH + 1, greet_z, 0)
    greet(*at(z, 1 - x_lo))

    @pl.when(slab > 0)
    def _():
        greet(view, slab - 1)

    @pl.when(slab < last)
    def _():
        greet(view, slab + 1)

    loads = [
        pltpu.make_async_copy(src, dst, load_sem.at[i])
        for i, (src, dst) in enumerate(
            (
                (proj_hbm, proj),
                (weight_hbm, weight),
                (rows_hbm, rowidx),
                (col_hbm, col),
                (frac_hbm, frac),
                (conj_hbm, conj_ref),
            )
        )
    ]
    for load in loads:
        load.start()

    loads[0].wait()
    for v in range(V):
        rows = proj[v].astype(F32)
        for r in range(R):
            stage[r * V + v : r * V + v + 1, :] = rows[r : r + 1]
    mine[...] = stage[...].astype(BF16)

    loads[3].wait()
    loads[4].wait()

    def prepare(tile, carry):
        off = pl.multiple_of(tile * TILE, TILE)
        k = col[:, pl.ds(off, TILE)].astype(F32)
        a = jnp.floor((k + 0.5) * (1.0 / STEP))
        place = k - a * STEP + frac[:, pl.ds(off, TILE)].astype(F32) * (1.0 / 256.0)
        for b in range(PARTS):
            fine[b, :, pl.ds(off, TILE)] = hat(place - b)
        lanes = iota((LANES, TILE), 0).astype(F32).astype(BF16)
        for v in range(V):
            coarse[v, :, pl.ds(off, TILE)] = hat(lanes - a[v : v + 1, :].astype(BF16)).astype(BF16)
        return carry

    early = jnp.where(z < 8, 12, jnp.where(z < 12, 2, 7))
    lax.fori_loop(0, early, prepare, 0)

    below, above = (slab > 0).astype(jnp.int32), (slab < last).astype(jnp.int32)
    pl.semaphore_wait(barrier, 4 * REACH + 2 + below + above)
    pair = pltpu.make_async_remote_copy(
        src_ref=mine,
        dst_ref=theirs,
        send_sem=pair_sem.at[0],
        recv_sem=pair_sem.at[1],
        device_id=partner,
        device_id_type=MESH,
    )
    pair.start()
    lax.fori_loop(early, NZ, prepare, 0)

    for b in range(PARTS):
        column = STEP * iota((W, LANES), 1) + b
        offset = column + iota((W, LANES), 0) - (W - 1)
        square = (offset * offset).astype(F32)
        odd = -1.0 / (math.pi * math.pi * jnp.maximum(square, 1.0))
        value = jnp.where(offset == 0, 0.25, jnp.where((offset & 1) == 1, odd, 0.0))
        ramp[:, b * LANES : (b + 1) * LANES] = jnp.where(column < W, value, 0.0).astype(BF16)

    flip = jnp.where(iota((W, W), 0) + iota((W, W), 1) == W - 1, 1.0, 0.0).astype(BF16)
    loads[1].wait()
    whole = weight[...]
    high = whole.astype(BF16).astype(F32)
    middle = (whole - high).astype(BF16).astype(F32)
    low = (whole - high - middle).astype(BF16).astype(F32)
    split = jnp.concatenate([high, middle, low], axis=0).astype(BF16)
    flipped = jnp.dot(split, flip, preferred_element_type=F32)
    mirror_weight[...] = flipped[0:V] + flipped[V : 2 * V] + flipped[2 * V : 3 * V]
    share = jnp.concatenate([mirror_weight[...]] * R, axis=0)

    kept[...] = (1.0 - share) * jnp.dot(mine[...], flip, preferred_element_type=F32)

    loads[2].wait()
    for t in range(NZ):
        blocks = []
        for v in range(V):
            wanted = jnp.broadcast_to(rowidx[v, t : t + 1, :], (2 * R, NZ))
            blocks.append(jnp.where(wanted == iota((2 * R, NZ), 0), 1.0, 0.0))
        pick[t] = jnp.concatenate(blocks, axis=0).T.astype(BF16)

    row, other = iota((V * R, V * R), 0), iota((V * R, V * R), 1)
    conj = jnp.zeros((V * R, V * R), jnp.int32)
    loads[5].wait()
    for v in range(V):
        conj = jnp.where((row & (V - 1)) == v, conj_ref[v], conj)
    same_row = (row >> 3) == (other >> 3)
    select = jnp.where(jnp.logical_and(same_row, (other & (V - 1)) == conj), 1.0, 0.0).astype(BF16)
    pair.wait_recv()
    chosen = jnp.dot(select, theirs[...], preferred_element_type=F32)
    blended = (kept[...] + share * chosen).astype(BF16)
    edge[...] = jnp.dot(blended, ramp[...], preferred_element_type=F32).astype(BF16)

    half = R * V // 2
    first_rows, last_rows = pl.ds(0, half), pl.ds(half, half)

    def halo_copy(i, src, dst, to):
        return pltpu.make_async_remote_copy(
            src_ref=edge.at[src],
            dst_ref=edge_in.at[dst],
            send_sem=halo_send.at[i],
            recv_sem=halo_recv.at[i],
            device_id=(view, to),
            device_id_type=MESH,
        )

    down = halo_copy(0, first_rows, last_rows, jnp.maximum(slab - 1, 0))
    up = halo_copy(1, last_rows, first_rows, jnp.minimum(slab + 1, last))

    @pl.when(slab > 0)
    def _():
        down.start()

    @pl.when(slab < last)
    def _():
        up.start()

    @pl.when(slab == 0)
    def _():
        edge_in[first_rows, :] = jnp.zeros((half, PARTS * LANES), BF16)

    @pl.when(slab == last)
    def _():
        edge_in[last_rows, :] = jnp.zeros((half, PARTS * LANES), BF16)

    inner = edge[...].astype(F32)
    for b in range(PARTS):
        band[b, half : half + R * V, :] = inner[:, b * LANES : (b + 1) * LANES]

    @pl.when(slab < last)
    def _():
        down.wait_recv()

    @pl.when(slab > 0)
    def _():
        up.wait_recv()

    outer = edge_in[...].astype(F32)
    for b in range(PARTS):
        band[b, 0:half, :] = outer[0:half, b * LANES : (b + 1) * LANES]
        band[b, half + R * V :, :] = outer[half:, b * LANES : (b + 1) * LANES]

    for v in range(V):
        lhs[v] = jnp.concatenate(
            [band[b, pl.ds(v, 2 * R, stride=V), :] for b in range(PARTS)], axis=0
        ).astype(BF16)

    def way(n):
        return 1 - 2 * lax.rem(n, 2)

    def distance(n):
        return NZ // 2 - (n + 1) // 2

    def tile_of(n):
        return lax.rem(z + NZ + way(n) * distance(n), NZ)

    def slot_of(n, hops):
        return (1 - way(n)) * REACH // 2 + hops - 1

    def to_relay(n):
        hops = distance(n) - REACH
        slot = slot_of(n, hops)
        return pltpu.make_async_remote_copy(
            src_ref=block.at[n],
            dst_ref=relay_in.at[slot],
            send_sem=block_send.at[n, 0],
            recv_sem=relay_recv.at[slot],
            device_id=at(lax.rem(z + NZ + way(n) * hops, NZ), x_lo),
            device_id_type=MESH,
        )

    def to_own(n, x):
        slot = slot_of(n, distance(n))
        return pltpu.make_async_remote_copy(
            src_ref=block.at[n, :, pl.ds(x * HALF, HALF)],
            dst_ref=z_in.at[slot, x_lo],
            send_sem=block_send.at[n, x],
            recv_sem=z_recv.at[slot, x_lo],
            device_id=at(tile_of(n), x),
            device_id_type=MESH,
        )

    my_half = pl.ds(pl.multiple_of(x_lo * HALF, HALF), HALF)
    to_x = pltpu.make_async_remote_copy(
        src_ref=block.at[NZ - 1, :, pl.ds(pl.multiple_of((1 - x_lo) * HALF, HALF), HALF)],
        dst_ref=x_in,
        send_sem=block_send.at[NZ - 1, 0],
        recv_sem=x_recv,
        device_id=at(z, 1 - x_lo),
        device_id_type=MESH,
    )

    def received(slot, x):
        pltpu.make_async_remote_copy(
            src_ref=block.at[0, :, pl.ds(0, HALF)],
            dst_ref=z_in.at[slot, x],
            send_sem=block_send.at[0, 0],
            recv_sem=z_recv.at[slot, x],
            device_id=at(z, 1 - x_lo),
            device_id_type=MESH,
        ).wait_recv()
        return z_in[slot, x].astype(F32)

    def interpolate(n, i):
        off = pl.multiple_of(tile_of(n) * TILE, TILE)
        for v in range(V):
            columns = jnp.dot(lhs[v], coarse[v, :, pl.ds(off, TILE)], preferred_element_type=F32)
            total = None
            for b in range(PARTS):
                weights = jnp.broadcast_to(fine[b, v : v + 1, pl.ds(off, TILE)], (2 * R, TILE))
                term = columns[b * 2 * R : (b + 1) * 2 * R] * weights
                total = term if total is None else total + term
            planes[i, v * 2 * R : (v + 1) * 2 * R, :] = total

    def picked(n, i):
        part[i] = jnp.dot(pick[tile_of(n)], planes[i].astype(BF16), preferred_element_type=F32)
        block[n] = part[i].astype(BF16)

    def step(m, carry):
        for i in range(2):
            interpolate(2 * m + i, i)
        for i in range(2):
            picked(2 * m + i, i)
        for i in range(2):
            n = 2 * m + i

            @pl.when(n < FAR)
            def _():
                to_relay(n).start()

            @pl.when(jnp.logical_and(n >= FAR, n < FAR + 2))
            def _():
                own[1 - i] = part[i]

            @pl.when(jnp.logical_and(n >= FAR + 2, n < NZ - 1))
            def _():
                for x in range(2):
                    to_own(n, x).start()

        return carry

    lax.fori_loop(0, NZ // 2, step, 0)
    to_x.start()

    for n, sources in ((FAR, (5, 3, 1)), (FAR + 1, (6, 4, 2, 0))):
        total = own[n - FAR]
        for source in sources:
            to_relay(source).wait_recv()
            total += relay_in[slot_of(source, distance(source) - REACH)].astype(F32)
        block[n] = total.astype(BF16)
        for x in range(2):
            to_own(n, x).start()

    def far_sent(n, carry):
        to_relay(n).wait_send()
        return carry

    def sent(n, carry):
        for x in range(2):
            to_own(n, x).wait_send()
        return carry

    lax.fori_loop(0, FAR, far_sent, 0)
    lax.fori_loop(FAR + 2, NZ - 1, sent, 0)

    to_x.wait_recv()
    total = part[1, :, my_half] + x_in[...].astype(F32)
    for n in (*range(FAR + 2, NZ - 1), FAR, FAR + 1):
        for x in range(2):
            total += received(slot_of(n, distance(n)), x)
    out_ref[...] = total * (1.0 / math.sqrt(V * lax.axis_size("view")))

    lax.fori_loop(FAR, FAR + 2, sent, 0)
    to_x.wait_send()
    pair.wait_send()

    @pl.when(slab > 0)
    def _():
        down.wait_send()

    @pl.when(slab < last)
    def _():
        up.wait_send()


def on_device(projections, conj_index, conj_weight, row_index, col_index, col_frac):
    pix = NZ * TILE
    anywhere = pl.BlockSpec(memory_space=pl.ANY)
    dma = pltpu.SemaphoreType.DMA
    return pl.pallas_call(
        kernel,
        out_shape=jax.ShapeDtypeStruct((NZ, HALF), F32),
        in_specs=[anywhere] * 6,
        out_specs=pl.BlockSpec(memory_space=pltpu.VMEM),
        scratch_shapes=[
            pltpu.SMEM((V,), jnp.int32),
            pltpu.VMEM((V, R, W), BF16),
            pltpu.VMEM((V, W), F32),
            pltpu.VMEM((V, NZ, NZ), jnp.int32),
            pltpu.VMEM((V, pix), jnp.int32),
            pltpu.VMEM((V, pix), jnp.int32),
            pltpu.VMEM((V * R, W), F32),
            pltpu.VMEM((V * R, W), BF16),
            pltpu.VMEM((V * R, W), BF16),
            pltpu.VMEM((V * R, W), F32),
            pltpu.VMEM((V, W), F32),
            pltpu.VMEM((W, PARTS * LANES), BF16),
            pltpu.VMEM((V * R, PARTS * LANES), BF16),
            pltpu.VMEM((V * R, PARTS * LANES), BF16),
            pltpu.VMEM((PARTS, 2 * R * V, LANES), F32),
            pltpu.VMEM((V, PARTS * 2 * R, LANES), BF16),
            pltpu.VMEM((V, LANES, pix), BF16),
            pltpu.VMEM((PARTS, V, pix), F32),
            pltpu.VMEM((NZ, NZ, 2 * R * V), BF16),
            pltpu.VMEM((2, 2 * R * V, TILE), F32),
            pltpu.VMEM((2, NZ, TILE), F32),
            pltpu.VMEM((2, NZ, TILE), F32),
            pltpu.VMEM((NZ, NZ, TILE), BF16),
            pltpu.VMEM((NZ, HALF), BF16),
            pltpu.VMEM((2 * REACH, NZ, TILE), BF16),
            pltpu.VMEM((2 * REACH, 2, NZ, HALF), BF16),
            dma((6,)),
            dma((2,)),
            dma((2,)),
            dma((2,)),
            dma((NZ, 2)),
            dma,
            dma((2 * REACH,)),
            dma((2 * REACH, 2)),
        ],
        compiler_params=pltpu.CompilerParams(
            collective_id=0, has_side_effects=True, vmem_limit_bytes=56 * 2**20
        ),
        name="backproject",
    )(conj_index, projections, conj_weight, row_index, col_index, col_frac)


def solution(mesh):
    return jax.shard_map(
        on_device,
        mesh=mesh,
        in_specs=(
            P("view", "slab", None),
            P("view"),
            P("view", None),
            P("view", None, "slab"),
            P("view", None),
            P("view", None),
        ),
        out_specs=P("slab", "view"),
        check_vma=False,
    )
```

time: 48.2 us -> 46.2 us (0.959)
  the two profiles are of different devices: /device:TPU:5 before, /device:TPU:6 now
where the time goes in v2:
time: 46.2 us; the launch traced here: 46 us
  Pallas kernels  44.6 us (97%)
  local copies, waits for them, and re-layouts  1.38 us (3%)
    pallas_call x1, Pallas kernels, on_device(): pl.pallas_call(kernel, out_shape=jax.ShapeDtypeStruct((NZ, HALF), F32), i...  44.6 us
    unnamed x1, local copies, waits for them, and re-layouts  1.38 us

profile of v2, /device:TPU:6, one launch (start us, length us, event | category | flops | bytes accessed | tf_op | source)
XLA Modules:
  0.0 46.0 jit_solution(4555895707991779765)
XLA Ops:
  0.0 44.6 %backproject.1 = f32[16,512]{1,0:T(8,128)} custom-call(s32[8]{0:T(128)} %conj_hbm.1, bf16[8,4,736]{2,1,0:T(4,128)(2,1)} %proj_hbm.1, f32[8,736]{1,0:T(8,128)} %weight_hbm.1, s32[8,16,16]{2,1,0:T(8,128)} %rows_hbm.1, s32[8,16384]{1,0:T(8,128)} %col_hbm.1, s32[8,16384]{1,0:T(8,128)} %frac_hbm.1), custom_call_target="tpu_custom_call" | custom-call | tf_op jit(solution)/shard_map/backproject/pallas_call | solution.py:403
  44.6 1.4 %copy.8 = f32[16,512]{1,0:T(8,128)} copy(f32[16,512]{1,0:T(8,128)} %backproject.1) | data formatting | bytes 65536

commit v3 on v2

--- a/solution.py
+++ b/solution.py
@@ -147,7 +147,7 @@
             coarse[v, :, pl.ds(off, TILE)] = hat(lanes - a[v : v + 1, :].astype(BF16)).astype(BF16)
         return carry
 
-    early = jnp.where(z < 8, 12, jnp.where(z < 12, 2, 7))
+    early = jnp.where(z < 8, 12, jnp.where(z < 12, 7, 10))
     lax.fori_loop(0, early, prepare, 0)
 
     below, above = (slab > 0).astype(jnp.int32), (slab < last).astype(jnp.int32)
@@ -355,14 +355,26 @@
     lax.fori_loop(0, NZ // 2, step, 0)
     to_x.start()
 
-    for n, sources in ((FAR, (5, 3, 1)), (FAR + 1, (6, 4, 2, 0))):
+    def relay(n):
         total = own[n - FAR]
-        for source in sources:
+        for source in range(n - 2, -1, -2):
             to_relay(source).wait_recv()
             total += relay_in[slot_of(source, distance(source) - REACH)].astype(F32)
         block[n] = total.astype(BF16)
         for x in range(2):
             to_own(n, x).start()
+
+    upper = z >= NZ // 2
+
+    @pl.when(upper)
+    def _():
+        relay(FAR + 1)
+        relay(FAR)
+
+    @pl.when(jnp.logical_not(upper))
+    def _():
+        relay(FAR)
+        relay(FAR + 1)
 
     def far_sent(n, carry):
         to_relay(n).wait_send()

time: 46.2 us -> 46.1 us (level); the launches traced: 46 us -> 45.2 us
  Pallas kernels: 44.6 us -> 43.8 us
    pallas_call x1, Pallas kernels: 44.6 us -> 43.8 us  [on_device(): pl.pallas_call(kernel, out_shape=jax.ShapeDtypeStruct((NZ, HALF), F32), i...]
where the time goes in v3:
time: 46.1 us; the launch traced here: 45.2 us
  Pallas kernels  43.8 us (95%)
  local copies, waits for them, and re-layouts  1.38 us (3%)
    pallas_call x1, Pallas kernels, on_device(): pl.pallas_call(kernel, out_shape=jax.ShapeDtypeStruct((NZ, HALF), F32), i...  43.8 us
    unnamed x1, local copies, waits for them, and re-layouts  1.38 us

profile of v3, /device:TPU:6, one launch (start us, length us, event | category | flops | bytes accessed | tf_op | source)
XLA Modules:
  0.0 45.2 jit_solution(4542814427054321883)
XLA Ops:
  0.0 43.8 %backproject.1 = f32[16,512]{1,0:T(8,128)} custom-call(s32[8]{0:T(128)} %conj_hbm.1, bf16[8,4,736]{2,1,0:T(4,128)(2,1)} %proj_hbm.1, f32[8,736]{1,0:T(8,128)} %weight_hbm.1, s32[8,16,16]{2,1,0:T(8,128)} %rows_hbm.1, s32[8,16384]{1,0:T(8,128)} %col_hbm.1, s32[8,16384]{1,0:T(8,128)} %frac_hbm.1), custom_call_target="tpu_custom_call" | custom-call | tf_op jit(solution)/shard_map/backproject/pallas_call | solution.py:415
  43.8 1.4 %copy.8 = f32[16,512]{1,0:T(8,128)} copy(f32[16,512]{1,0:T(8,128)} %backproject.1) | data formatting | bytes 65536
